TPU v7x, 256 devices: a whole 4x4x8 slice. The times are simulated.
256 devices in a mesh: dp: 32 (over y, z_hi, core), tensor: 8 (over x, z_lo).
Axes of the slice: x: 4, y: 4, z: 8 (z_hi: 4, z_lo: 2; z = z_hi * 2 + z_lo), core: 2. Of those that a mesh axis runs over, the one named last changes fastest.
Arguments:
- student_hidden: bfloat16 [32768, 3584], P(('dp', 'tensor')), may hold values from -140 to 140
- norm_gain: float32 [3584], replicated, may hold values from 0.1 to 1.9
- projection: bfloat16 [3584, 4096], P('dp', 'tensor'), may hold values from -0.09375 to 0.09375
- teacher_terms: bfloat16 [8, 32768, 4096], P('tensor', 'dp'), may hold values from -80 to 80
Outputs:
- distill_loss: float32 [], replicated
- hidden_grad: bfloat16 [32768, 3584], P(('dp', 'tensor'))
- projection_update: float32 [3584, 4096], P('dp', 'tensor')
- gain_update: float32 [3584], replicated
All inputs are finite; a program needn't handle non-finite values.
Results may differ from a plain program's by a relative error of at most 0.028.
Values may be sent and summed in bfloat16 or wider, within the bound.
A program may use at most 64 MiB of HBM per device.

v0:
```python
import jax
import jax.numpy as jnp
from jax import lax
from jax.experimental import pallas as pl
from jax.experimental.pallas import tpu as pltpu
from jax.sharding import PartitionSpec as P

epsilon = 1e-06
MESH = pl.DeviceIdType.MESH
F32 = jnp.float32
BF16 = jnp.bfloat16

ROWS = 128
DS = 3584
PR = 112
PC = 512
DT = 4096
FX = 1024
HP = 256
HALF = DS // 2
YR = DS // 4
N_MSG = 160


def kernel(
    hid, gain_in, proj, teach,
    loss_out, hid_out, proj_out, gain_out,
    norm_all, norm_t, proj_full,
    t_ma, t_mb, t_own, t_z,
    z_in, x_fl, x_fr, x_gl, x_gr, x_sum, z_in2, s_fl, s_fr, s_gl, s_gr,
    pred, pgrad,
    pg, c_in, y_fl, y_fr, y_gl, y_gr, y_sum, zd_in,
    ng, n_fl, n_fr, n_gl, n_gr,
    gain, gain_t, m_1, m_2, s_1, s_2,
    send_sem, recv_sem, local_sem,
):
    dp = lax.axis_index("dp")
    tp = lax.axis_index("tensor")
    y, zh, c = dp // 8, (dp // 2) % 4, dp % 2
    x, zl = tp // 2, tp % 2
    z = zh * 2 + zl

    def device(y=y, z=z, c=c, x=x):
        return ((y * 4 + z // 2) * 2 + c, x * 2 + z % 2)

    def xp(d):
        return (x + d) % 4

    def yp(d):
        return (y + d) % 4

    def zp(d):
        return (z + d) % 8

    right, left = device(x=xp(1)), device(x=xp(3))
    up, down = device(y=yp(1)), device(y=yp(3))
    above, below = device(z=zp(1)), device(z=zp(7))
    mate = device(c=1 - c)
    pair = device(z=z + 1 - 2 * zl)

    opened = []

    def send(src, dst, dev):
        i = len(opened)
        copy = pltpu.make_async_remote_copy(
            src_ref=src, dst_ref=dst, send_sem=send_sem.at[i], recv_sem=recv_sem.at[i],
            device_id=dev, device_id_type=MESH,
        )
        copy.start()
        opened.append(copy)
        return copy

    n_local = [0]

    def fetch(src, dst):
        copy = pltpu.make_async_copy(src, dst, local_sem.at[n_local[0]])
        n_local[0] += 1
        copy.start()
        return copy

    def arrived(*copies):
        for copy in copies:
            copy.wait_recv()

    def merge(out, parts, n):
        def step(i, _):
            total = parts[0][i].astype(F32)
            for part in parts[1:]:
                total = total + part[i].astype(F32)
            out[i] = total.astype(out.dtype)
            return 0
        lax.fori_loop(0, n, step, 0)

    def merge_rows(out, parts, n):
        def step(i, _):
            rows = pl.ds(pl.multiple_of(i * 16, 16), 16)
            total = parts[0][rows, :].astype(F32)
            for part in parts[1:]:
                total = total + part[rows, :].astype(F32)
            out[rows, :] = total.astype(out.dtype)
            return 0
        lax.fori_loop(0, n // 16, step, 0)

    def transpose(t):
        out_cols = slice(t * ROWS, t * ROWS + ROWS)

        def step(i, _):
            cols = pl.ds(pl.multiple_of(i * 512, 512), 512)
            norm_t[cols, out_cols] = norm_all[t, :, cols].T
            return 0

        lax.fori_loop(0, DS // 512, step, 0)

    places = (0, 1, 3, 2)

    def pred_part(part, first, end):
        rows = slice(first * ROWS, end * ROWS)

        def step(k, _):
            cols = pl.ds(pl.multiple_of(k * PC + part * HP, HP), HP)
            out_cols = pl.ds(pl.multiple_of(part * PC + k * HP, HP), HP)
            rows_part = norm_all[first:end].reshape((end - first) * ROWS, DS)
            cols_part = proj_full[:, :, :, :, cols].reshape(DS, HP)
            product = jnp.dot(rows_part, cols_part, preferred_element_type=F32)
            pred[rows, out_cols] = product.astype(BF16)
            return 0

        lax.fori_loop(0, 2, step, 0)

    group_1 = [(dc, dz) for dc in range(2) for dz in range(8) if dc or dz]
    group_2 = [(dx, dy) for dx in range(4) for dy in range(4) if dx or dy]
    peers_1 = [device(c=(c + dc) % 2, z=zp(dz)) for dc, dz in group_1]
    peers_2 = [device(x=xp(dx), y=yp(dy)) for dx, dy in group_2]
    barrier = pltpu.get_barrier_semaphore()
    for dev in peers_1 + peers_2:
        pl.semaphore_signal(barrier, inc=1, device_id=dev, device_id_type=MESH)
    pl.semaphore_wait(barrier, len(peers_1) + len(peers_2))

    def tcols(d, part, k):
        return pl.ds(pl.multiple_of(xp(d) * FX + k * PC + part * HP, HP), HP)

    def raw(t, d, part, dst, dev):
        return [send(teach.at[:, t, :, tcols(d, part, k)], dst.at[:, :, pl.ds(k * HP, HP)], dev)
                for k in range(2)]

    def load(t, d, part, dst):
        return [fetch(teach.at[:, t, :, tcols(d, part, k)], dst.at[:, :, pl.ds(k * HP, HP)])
                for k in range(2)]

    def pblock(zz):
        return proj_full.at[y, zz // 2, c, :, pl.ds(pl.multiple_of((zz % 2) * PC, PC), PC)]

    ups = [send(proj, pblock(z), above)]
    dns = [send(proj, pblock(z), below)]
    x_fwd_r = raw(0, 2, 1, x_fl, right)
    x_fwd_l = raw(1, 2, 1, x_fr, left)
    order = (2, 1, 3, 0)
    z_msgs = []
    own = fetch(proj, pblock(z))
    load_ma = load(0, 1, 1, t_ma)
    load_mb = load(1, 3, 1, t_mb)
    load_z = [load(zl, d, 0, t_z.at[k]) for k, d in enumerate(order)]
    load_own = load(0, 0, 1, t_own.at[0]) + load(1, 0, 1, t_own.at[1])

    for i in range(DS // 128):
        gain[:, i * 128:(i + 1) * 128] = gain_in[i * 128:(i + 1) * 128].reshape(1, 128)

    def norm_step(i, _):
        rows = pl.ds(pl.multiple_of(i * 16, 16), 16)
        h = hid[rows, :].astype(F32)
        inv = lax.rsqrt(jnp.mean(h * h, axis=1, keepdims=True) + epsilon)
        norm_all[0, rows, :] = (h * inv * gain[...]).astype(BF16)
        return 0

    lax.fori_loop(0, ROWS // 16, norm_step, 0)
    n_r = send(norm_all.at[0], norm_all.at[2], right)
    n_l = send(norm_all.at[0], norm_all.at[1], left)
    for i in range(32):
        gain_t[i:i + 1, 0:PR] = gain[:, i * PR:(i + 1) * PR]

    for s in range(1, 4):
        ups[-1].wait_recv()
        ups.append(send(pblock(zp(8 - s)), pblock(zp(8 - s)), above))
        dns[-1].wait_recv()
        if s < 3:
            dns.append(send(pblock(zp(s)), pblock(zp(s)), below))
        if s == 2:
            z_msgs.append(raw(1 - zl, 2, 0, z_in.at[0], pair))
    arrived(*x_fwd_r)
    for copy in load_ma:
        copy.wait()
    merge(t_ma, (t_ma, x_fl), 4)
    x_last = [send(t_ma, x_gl.at[0], right)]
    arrived(*x_fwd_l)
    for copy in load_mb:
        copy.wait()
    merge(t_mb, (t_mb, x_fr), 4)
    x_last += [send(t_mb, x_gr.at[1], left)]
    x_last += raw(1, 1, 1, x_gl.at[1], right)
    x_last += raw(0, 3, 1, x_gr.at[0], left)
    z_msgs.append(raw(1 - zl, 1, 0, z_in.at[1], pair))
    ups[-1].wait_recv()
    own.wait()
    y_up = send(proj_full.at[y, :, c], proj_full.at[y, :, c], up)
    y_dn = send(proj_full.at[y, :, c], proj_full.at[y, :, c], down)
    core = [send(proj_full.at[y, :, c], proj_full.at[y, :, c], mate)]
    z_msgs.append(raw(1 - zl, 3, 0, z_in.at[2], pair))

    transpose(0)
    a, b = pl.ds(0, 2), pl.ds(2, 2)

    def z_merge(k):
        arrived(*z_msgs[k])
        for copy in load_z[k]:
            copy.wait()
        merge(t_z.at[k], (t_z.at[k], z_in.at[k]), 4)

    z_merge(0)
    z_msgs.append(raw(1 - zl, 0, 0, z_in.at[3], pair))

    y_up.wait_recv()
    y_up2 = send(proj_full.at[yp(3), a, c], proj_full.at[yp(3), a, c], up)
    core.append(send(proj_full.at[yp(3), :, c], proj_full.at[yp(3), :, c], mate))
    y_dn.wait_recv()
    y_dn2 = send(proj_full.at[yp(1), b, c], proj_full.at[yp(1), b, c], down)
    core.append(send(proj_full.at[yp(1), :, c], proj_full.at[yp(1), :, c], mate))

    lo, hi = pl.ds(0, ROWS // 2), pl.ds(ROWS // 2, ROWS // 2)
    n_r.wait_recv()
    n_r2 = send(norm_all.at[2, lo], norm_all.at[3, lo], right)
    n_l.wait_recv()
    n_l2 = send(norm_all.at[1, hi], norm_all.at[3, hi], left)
    transpose(1)
    transpose(2)
    z_merge(1)
    z_merge(2)
    arrived(*x_last)
    for copy in load_own:
        copy.wait()
    for t in range(2):
        merge(x_sum.at[t], (t_own.at[t], x_gl.at[t], x_gr.at[t]), 4)
    z_msg2 = send(x_sum.at[1 - zl], z_in2, pair)
    s_fwd_r = send(t_z.at[0, a], s_fl, right)
    s_fwd_l = send(t_z.at[0, b], s_fr, left)


    y_up2.wait_recv()
    y_dn2.wait_recv()
    core.append(send(proj_full.at[yp(2), :, c], proj_full.at[yp(2), :, c], mate))
    arrived(*core)
    pred_part(1, 0, 3)
    pred_part(0, 0, 3)
    arrived(n_r2, n_l2)

    s_last = [send(t_z.at[1, b], s_gl.at[b], right)]
    s_last += [send(t_z.at[2, a], s_gr.at[a], left)]

    transpose(3)
    pred_part(1, 3, 4)
    pred_part(0, 3, 4)

    def mismatch_part(part, terms):
        cols = slice(part * PC, part * PC + PC)

        total = jnp.zeros((1, PC), F32)
        for p in range(4):
            t = xp(places[p])

            def step(i, loss):
                rows = pl.ds(pl.multiple_of(i * 16, 16), 16)
                out_rows = pl.ds(pl.multiple_of(p * ROWS + i * 16, 16), 16)
                target = terms[0][t, rows, :].astype(F32)
                for term in terms[1:]:
                    target = target + term[t, rows, :].astype(F32)
                miss = pred[out_rows, cols].astype(F32) - target
                pgrad[out_rows, cols] = miss.astype(BF16)
                return loss + jnp.sum(miss * miss, axis=0, keepdims=True)

            total = lax.fori_loop(0, ROWS // 16, step, total)
        return total

    def ngrad_half(part, k):
        def step(i, _):
            yy = 2 * k + i
            cols = pl.ds(pl.multiple_of(yy * YR, 128), YR)
            total = jnp.zeros((4 * ROWS, YR), F32)
            for m in range(2):
                weights = proj_full[yy, :, :, :, m * PC + part * HP:m * PC + part * HP + HP]
                total = total + lax.dot_general(
                    pgrad[:, part * PC + m * HP:part * PC + m * HP + HP],
                    weights.reshape(YR, HP), (((1,), (1,)), ((), ())),
                    preferred_element_type=F32)
            total = total.reshape(4, ROWS, YR)
            if part == 0:
                total = total + ng[:, :, cols].astype(F32)
            ng[:, :, cols] = total.astype(BF16)
            return 0

        lax.fori_loop(0, 2, step, 0)

    y2, y1, y3 = yp(2), yp(1), yp(3)

    def pgrad_block(q, yy):
        rows = pl.ds(pl.multiple_of(yy * YR, 128), YR)
        product = jnp.dot(norm_t[rows, :], pgrad[:, q * PC:q * PC + PC], preferred_element_type=F32)
        pg[q, yy] = product.astype(BF16).reshape(4, 2, PR, PC)
        return send(pg.at[q, yy, :, 1 - c], c_in.at[q, yy], mate)

    def core_merge(q, copy, yy):
        copy.wait_recv()
        merge(c_in.at[q, yy], (c_in.at[q, yy], pg.at[q, yy, :, c]), 4)

    def pgrad_sends(q):
        c_2 = pgrad_block(q, y2)
        c_1 = pgrad_block(q, y1)
        c_3 = pgrad_block(q, y3)
        c_0 = pgrad_block(q, y)
        core_merge(q, c_2, y2)
        fwd_u = send(c_in.at[q, y2, a], y_fl.at[q], up)
        fwd_d = send(c_in.at[q, y2, b], y_fr.at[q], down)
        core_merge(q, c_1, y1)
        dir_u = send(c_in.at[q, y1, b], y_gl.at[q, b], up)
        core_merge(q, c_3, y3)
        dir_d = send(c_in.at[q, y3, a], y_gr.at[q, a], down)
        core_merge(q, c_0, y)
        return fwd_u, fwd_d, dir_u, dir_d

    def y_merge(q, fwd_u, fwd_d, dir_u, dir_d):
        fwd_u.wait_recv()
        merge(c_in.at[q, y1, a], (c_in.at[q, y1, a], y_fl.at[q]), 2)
        mrg_u = send(c_in.at[q, y1, a], y_gl.at[q, a], up)
        fwd_d.wait_recv()
        merge(c_in.at[q, y3, b], (c_in.at[q, y3, b], y_fr.at[q]), 2)
        mrg_d = send(c_in.at[q, y3, b], y_gr.at[q, b], down)
        return dir_u, dir_d, mrg_u, mrg_d

    def sblock(q, d):
        zz = zp(d)
        return y_sum.at[q, zz // 2, :, pl.ds(pl.multiple_of((zz % 2) * HP, HP), HP)]

    def z_sends(q, copies):
        arrived(*copies)
        merge(y_sum.at[q], (c_in.at[q, y], y_gl.at[q], y_gr.at[q]), 4)
        return [send(sblock(q, d), zd_in.at[q, d - 1], device(z=zp(d)))
                for d in (4, 3, 5, 2, 6, 1, 7)]

    s_fwd_r.wait_recv()
    merge(t_z.at[1, a], (t_z.at[1, a], s_fl), 2)
    s_last += [send(t_z.at[1, a], s_gl.at[a], right)]
    s_fwd_l.wait_recv()
    merge(t_z.at[2, b], (t_z.at[2, b], s_fr), 2)
    s_last += [send(t_z.at[2, b], s_gr.at[b], left)]
    z_msg2.wait_recv()
    loss = mismatch_part(1, (x_sum.at[zl], z_in2))
    y_1 = pgrad_sends(1)
    ngrad_half(1, 0)
    ngrad_half(1, 1)
    y_1 = y_merge(1, *y_1)

    arrived(*z_msgs[3])
    for copy in load_z[3]:
        copy.wait()
    arrived(*s_last)
    loss = loss + mismatch_part(0, (t_z.at[3], z_in.at[3], s_gl, s_gr))
    loss = jnp.sum(loss, axis=1, keepdims=True)
    ca, cb = pl.ds(0, HALF), pl.ds(HALF, HALF)
    y_0 = pgrad_sends(0)
    ngrad_half(0, 0)
    n_fwd_r = send(ng.at[3, :, ca], n_fl, right)
    n_last = [send(ng.at[2, :, ca], n_gr.at[:, ca], left)]
    ngrad_half(0, 1)
    n_fwd_l = send(ng.at[3, :, cb], n_fr, left)
    n_last += [send(ng.at[1, :, cb], n_gl.at[:, cb], right)]
    y_0 = y_merge(0, *y_0)
    z_1 = z_sends(1, y_1)
    n_fwd_r.wait_recv()
    merge_rows(ng.at[1, :, ca], (ng.at[1, :, ca], n_fl), ROWS)
    n_last += [send(ng.at[1, :, ca], n_gl.at[:, ca], right)]
    z_0 = z_sends(0, y_0)
    n_fwd_l.wait_recv()
    merge_rows(ng.at[2, :, cb], (ng.at[2, :, cb], n_fr), ROWS)
    n_last += [send(ng.at[2, :, cb], n_gr.at[:, cb], left)]
    squares = jnp.zeros((PR, HP), F32)
    gains = jnp.zeros((PR, HP), F32)
    for q, copies in ((1, z_1), (0, z_0)):
        arrived(*copies)
        block = sblock(q, 0)[...].astype(F32)
        for d in range(7):
            block = block + zd_in[q, d].astype(F32)
        cols = slice(q * HP, q * HP + HP)
        proj_out[:, cols] = block
        squares = squares + block * block
        gains = gains + block * proj[:, cols].astype(F32)
    squares = jnp.sum(jnp.sum(squares, axis=0, keepdims=True), axis=1, keepdims=True)
    gains = gains[:, :128] + gains[:, 128:]
    gains = jnp.concatenate([gains, jnp.zeros((128 - PR, 128), F32)], axis=0)
    gains = jnp.sum(gains.T, axis=0, keepdims=True)

    row = lax.broadcasted_iota(jnp.int32, (8, 128), 0)
    pack = jnp.where(row == 0, gains, jnp.where(row == 1, squares, jnp.where(row == 2, loss, 0.0)))
    m_1[...] = pack
    s_1[c * 8 + z] = pack
    small = [send(m_1, s_1.at[c * 8 + z], dev) for dev in peers_1]
    arrived(*small)
    total = s_1[0]
    for i in range(1, 16):
        total = total + s_1[i]
    for i in range(4):
        for k in range(2):
            m_2[i * 2 + k:i * 2 + k + 1, :] = s_1[k * 8 + 2 * i, 0:1, :] + s_1[k * 8 + 2 * i + 1, 0:1, :]
    m_2[8:16, :] = total
    s_2[x * 4 + y] = m_2[...]
    small = [send(m_2, s_2.at[x * 4 + y], dev) for dev in peers_2]

    arrived(*n_last)

    def hid_step(i, _):
        rows = pl.ds(pl.multiple_of(i * 16, 16), 16)
        g = ng[0, rows, :].astype(F32) + n_gl[rows, :].astype(F32) + n_gr[rows, :].astype(F32)
        h = hid[rows, :].astype(F32)
        inv = lax.rsqrt(jnp.mean(h * h, axis=1, keepdims=True) + epsilon)
        scaled = h * inv
        g = g * gain[...]
        mean = jnp.mean(g * scaled, axis=1, keepdims=True)
        hid_out[rows, :] = (inv * (g - scaled * mean)).astype(BF16)
        return 0

    lax.fori_loop(0, ROWS // 16, hid_step, 0)

    arrived(*small)
    total = s_2[0, 8:16, :]
    for i in range(1, 16):
        total = total + s_2[i, 8:16, :]
    gain_grads = []
    gain_squares = jnp.zeros((1, 1), F32)
    for k in range(4):
        block = s_2[k, 0:8, :] + s_2[4 + k, 0:8, :] + s_2[8 + k, 0:8, :] + s_2[12 + k, 0:8, :]
        block = block[:, 0:PR] / gain_t[8 * k:8 * k + 8, 0:PR]
        gain_grads.append(block)
        gain_squares = gain_squares + jnp.sum(
            jnp.sum(block * block, axis=0, keepdims=True), axis=1, keepdims=True)
    factor = lax.rsqrt((total[1:2, 0:1] + gain_squares) / (DS * DT + DS) + epsilon)
    proj_out[...] = proj_out[...] * factor
    for k in range(4):
        gain_out[8 * k:8 * k + 8, :] = gain_grads[k] * factor
    loss_out[...] = total[2:3, :] / (32768 * DT)

    for copy in opened:
        copy.wait_send()


def finish(loss, hid, proj, gain, loss_out, hid_out, proj_out, gain_out, row, block, sem):
    parts = [pl.ds(i * 32, 32) for i in range(4)]
    loads = [pltpu.make_async_copy(hid.at[p], block.at[p], sem.at[i]) for i, p in enumerate(parts)]
    for copy in loads:
        copy.start()
    proj_out[...] = proj[...]
    loss_out[...] = loss[...]
    for i in range(32):
        row[:, i * PR:(i + 1) * PR] = gain[i:i + 1, :]
    for i in range(DS // 128):
        gain_out[i * 128:(i + 1) * 128] = row[0, i * 128:(i + 1) * 128]
    stores = []
    for i, p in enumerate(parts):
        loads[i].wait()
        stores.append(pltpu.make_async_copy(block.at[p], hid_out.at[p], sem.at[4 + i]))
        stores[i].start()
    for copy in stores:
        copy.wait()


def shards(student_hidden, norm_gain, projection, teacher_terms):
    teach = teacher_terms.reshape(4, 2, ROWS, DT)
    vmem = pl.BlockSpec(memory_space=pltpu.VMEM)
    V = pltpu.VMEM
    loss, hidden_grad, projection_update, gain_update = pl.pallas_call(
        kernel,
        out_shape=(
            jax.ShapeDtypeStruct((1, 128), F32),
            jax.ShapeDtypeStruct((ROWS, DS), BF16),
            jax.ShapeDtypeStruct((PR, PC), F32),
            jax.ShapeDtypeStruct((32, PR), F32),
        ),
        in_specs=[vmem, vmem, vmem, pl.BlockSpec(memory_space=pl.ANY)],
        out_specs=(vmem,) * 4,
        scratch_shapes=[
            V((4, ROWS, DS), BF16), V((DS, 4 * ROWS), BF16), V((4, 4, 2, PR, FX), BF16),
            V((4, ROWS, PC), BF16), V((4, ROWS, PC), BF16), V((2, 4, ROWS, PC), BF16),
            V((4, 4, ROWS, PC), BF16),
            V((4, 4, ROWS, PC), BF16),
            V((4, ROWS, PC), BF16), V((4, ROWS, PC), BF16),
            V((2, 4, ROWS, PC), BF16), V((2, 4, ROWS, PC), BF16), V((2, 4, ROWS, PC), BF16),
            V((4, ROWS, PC), BF16),
            V((2, ROWS, PC), BF16), V((2, ROWS, PC), BF16),
            V((4, ROWS, PC), BF16), V((4, ROWS, PC), BF16),
            V((4 * ROWS, FX), BF16), V((4 * ROWS, FX), BF16),
            V((2, 4, 4, 2, PR, PC), BF16), V((2, 4, 4, PR, PC), BF16),
            V((2, 2, PR, PC), BF16), V((2, 2, PR, PC), BF16),
            V((2, 4, PR, PC), BF16), V((2, 4, PR, PC), BF16), V((2, 4, PR, PC), BF16),
            V((2, 7, PR, HP), BF16),
            V((4, ROWS, DS), BF16), V((ROWS, HALF), BF16), V((ROWS, HALF), BF16),
            V((ROWS, DS), BF16), V((ROWS, DS), BF16),
            V((1, DS), F32), V((32, 128), F32), V((8, 128), F32), V((16, 128), F32),
            V((16, 8, 128), F32), V((16, 16, 128), F32),
            pltpu.SemaphoreType.DMA((N_MSG,)), pltpu.SemaphoreType.DMA((N_MSG,)),
            pltpu.SemaphoreType.DMA((24,)),
        ],
        compiler_params=pltpu.CompilerParams(
            collective_id=0, has_side_effects=True, vmem_limit_bytes=62 * 1024 * 1024
        ),
    )(student_hidden, norm_gain, projection, teach)
    loss, hidden_grad, projection_update, gain_update = pl.pallas_call(
        finish,
        out_shape=(
            jax.ShapeDtypeStruct((1, 128), F32),
            jax.ShapeDtypeStruct((ROWS, DS), BF16),
            jax.ShapeDtypeStruct((PR, PC), F32),
            jax.ShapeDtypeStruct((DS,), F32),
        ),
        in_specs=[vmem, pl.BlockSpec(memory_space=pl.ANY), vmem, vmem],
        out_specs=(vmem, pl.BlockSpec(memory_space=pl.ANY), vmem, vmem),
        scratch_shapes=[V((1, DS), F32), V((ROWS, DS), BF16), pltpu.SemaphoreType.DMA((8,))],
        compiler_params=pltpu.CompilerParams(vmem_limit_bytes=62 * 1024 * 1024),
    )(loss, hidden_grad, projection_update, gain_update)
    return loss[0, 0], hidden_grad, projection_update, gain_update


def solution(mesh):
    in_specs = (P(("dp", "tensor"), None), P(), P("dp", "tensor"), P("tensor", "dp", None))
    out_specs = (P(), P(("dp", "tensor"), None), P("dp", "tensor"), P())
    return jax.shard_map(shards, mesh=mesh, in_specs=in_specs, out_specs=out_specs, check_vma=False)
```

profile of v0, /device:TPU:1, one launch (start us, length us, event | category | flops | bytes accessed | tf_op | source)
XLA Modules:
  0.0 149.1 jit_solution(3614082294462482972)
XLA Ops:
  0.6 144.8 %shard_map.75 = (f32[1,128]{1,0:T(1,128)}, bf16[128,3584]{1,0:T(8,128)(2,1)}, f32[112,512]{1,0:T(8,128)}, f32[32,112]{1,0:T(8,128)}) custom-call(bf16[128,3584]{1,0:T(8,128)(2,1)} %hid.1, f32[3584]{0:T(1024)} %gain_in.1, bf16[112,512]{1,0:T(8,128)(2,1)} %proj.1, bf16[4,2,128,4096]{3,2,1,0:T(8,128)(2,1)} %bitcast.3), custom_call_target="tpu_custom_call" | custom-call | tf_op jit(solution)/shard_map/pallas_call | solution.py:476
  145.4 3.7 %shard_map.76 = (f32[1,128]{1,0:T(1,128)}, bf16[128,3584]{1,0:T(8,128)(2,1)}, f32[112,512]{1,0:T(8,128)}, f32[3584]{0:T(1024)}) custom-call(f32[1,128]{1,0:T(1,128)} %get-tuple-element.12.loss, bf16[128,3584]{1,0:T(8,128)(2,1)} %get-tuple-element.13.hid, f32[112,512]{1,0:T(8,128)} %get-tuple-element.14.proj, f32[32,112]{1,0:T(8,128)} %get-tuple-element.15.gain), custom_call_target="tpu_custom_call" | custom-call | tf_op jit(solution)/shard_map/pallas_call | solution.py:512
where the time goes:
time: 149 us
  Pallas kernels  148 us (99%)
    pallas_call x1, Pallas kernels, shards(): pl.pallas_call(kernel, out_shape=(jax.ShapeDtypeStruct((1, 128), F32), ja...  145 us
    pallas_call x1, Pallas kernels, shards(): pl.pallas_call(finish, out_shape=(jax.ShapeDtypeStruct((1, 128), F32), ja...  3.67 us

commit v1 on v0

--- a/solution.py
+++ b/solution.py
@@ -29,7 +29,7 @@
     t_ma, t_mb, t_own, t_z,
     z_in, x_fl, x_fr, x_gl, x_gr, x_sum, z_in2, s_fl, s_fr, s_gl, s_gr,
     pred, pgrad,
-    pg, c_in, y_fl, y_fr, y_gl, y_gr, y_sum, zd_in,
+    pg, c_in, y_fl, y_fr, y_gl, y_gr, y_sum, zd_in, zf_in,
     ng, n_fl, n_fr, n_gl, n_gr,
     gain, gain_t, m_1, m_2, s_1, s_2,
     send_sem, recv_sem, local_sem,
@@ -237,9 +237,10 @@
     arrived(*x_last)
     for copy in load_own:
         copy.wait()
-    for t in range(2):
-        merge(x_sum.at[t], (t_own.at[t], x_gl.at[t], x_gr.at[t]), 4)
-    z_msg2 = send(x_sum.at[1 - zl], z_in2, pair)
+    other = 1 - zl
+    merge(x_sum.at[other], (t_own.at[other], x_gl.at[other], x_gr.at[other]), 4)
+    z_msg2 = send(x_sum.at[other], z_in2, pair)
+    merge(x_sum.at[zl], (t_own.at[zl], x_gl.at[zl], x_gr.at[zl]), 4)
     s_fwd_r = send(t_z.at[0, a], s_fl, right)
     s_fwd_l = send(t_z.at[0, b], s_fr, left)
 
@@ -257,7 +258,6 @@
 
     transpose(3)
     pred_part(1, 3, 4)
-    pred_part(0, 3, 4)
 
     def mismatch_part(part, terms):
         cols = slice(part * PC, part * PC + PC)
@@ -310,20 +310,20 @@
         copy.wait_recv()
         merge(c_in.at[q, yy], (c_in.at[q, yy], pg.at[q, yy, :, c]), 4)
 
-    def pgrad_sends(q):
-        c_2 = pgrad_block(q, y2)
-        c_1 = pgrad_block(q, y1)
-        c_3 = pgrad_block(q, y3)
-        c_0 = pgrad_block(q, y)
+    def pgrad_begin(q):
+        return pgrad_block(q, y2), pgrad_block(q, y1)
+
+    def pgrad_sends(q, c_2, c_1):
         core_merge(q, c_2, y2)
         fwd_u = send(c_in.at[q, y2, a], y_fl.at[q], up)
         fwd_d = send(c_in.at[q, y2, b], y_fr.at[q], down)
+        c_3 = pgrad_block(q, y3)
         core_merge(q, c_1, y1)
         dir_u = send(c_in.at[q, y1, b], y_gl.at[q, b], up)
+        c_0 = pgrad_block(q, y)
         core_merge(q, c_3, y3)
         dir_d = send(c_in.at[q, y3, a], y_gr.at[q, a], down)
-        core_merge(q, c_0, y)
-        return fwd_u, fwd_d, dir_u, dir_d
+        return (fwd_u, fwd_d, dir_u, dir_d), c_0
 
     def y_merge(q, fwd_u, fwd_d, dir_u, dir_d):
         fwd_u.wait_recv()
@@ -341,21 +341,30 @@
     def z_sends(q, copies):
         arrived(*copies)
         merge(y_sum.at[q], (c_in.at[q, y], y_gl.at[q], y_gr.at[q]), 4)
-        return [send(sblock(q, d), zd_in.at[q, d - 1], device(z=zp(d)))
-                for d in (4, 3, 5, 2, 6, 1, 7)]
-
+        far = send(sblock(q, 4), zf_in.at[q], below)
+        near = [send(sblock(q, d), zd_in.at[q, d - 1], device(z=zp(d))) for d in (3, 2, 6, 1, 7)]
+        return far, near
+
+    def z_finish(q, far, near):
+        far.wait_recv()
+        block = sblock(q, 5)
+        block[...] = (block[...].astype(F32) + zf_in[q].astype(F32)).astype(BF16)
+        return near + [send(block, zd_in.at[q, 4], device(z=zp(5)))]
+
+    z_msg2.wait_recv()
+    loss = mismatch_part(1, (x_sum.at[zl], z_in2))
+    begun = pgrad_begin(1)
+    pred_part(0, 3, 4)
     s_fwd_r.wait_recv()
     merge(t_z.at[1, a], (t_z.at[1, a], s_fl), 2)
     s_last += [send(t_z.at[1, a], s_gl.at[a], right)]
     s_fwd_l.wait_recv()
     merge(t_z.at[2, b], (t_z.at[2, b], s_fr), 2)
     s_last += [send(t_z.at[2, b], s_gr.at[b], left)]
-    z_msg2.wait_recv()
-    loss = mismatch_part(1, (x_sum.at[zl], z_in2))
-    y_1 = pgrad_sends(1)
+    y_1, own_1 = pgrad_sends(1, *begun)
     ngrad_half(1, 0)
     ngrad_half(1, 1)
-    y_1 = y_merge(1, *y_1)
+    core_merge(1, own_1, y)
 
     arrived(*z_msgs[3])
     for copy in load_z[3]:
@@ -364,15 +373,19 @@
     loss = loss + mismatch_part(0, (t_z.at[3], z_in.at[3], s_gl, s_gr))
     loss = jnp.sum(loss, axis=1, keepdims=True)
     ca, cb = pl.ds(0, HALF), pl.ds(HALF, HALF)
-    y_0 = pgrad_sends(0)
+    begun = pgrad_begin(0)
+    y_1 = y_merge(1, *y_1)
+    y_0, own_0 = pgrad_sends(0, *begun)
     ngrad_half(0, 0)
     n_fwd_r = send(ng.at[3, :, ca], n_fl, right)
     n_last = [send(ng.at[2, :, ca], n_gr.at[:, ca], left)]
     ngrad_half(0, 1)
     n_fwd_l = send(ng.at[3, :, cb], n_fr, left)
     n_last += [send(ng.at[1, :, cb], n_gl.at[:, cb], right)]
+    core_merge(0, own_0, y)
+    z_1 = z_sends(1, y_1)
     y_0 = y_merge(0, *y_0)
-    z_1 = z_sends(1, y_1)
+    z_1 = z_finish(1, *z_1)
     n_fwd_r.wait_recv()
     merge_rows(ng.at[1, :, ca], (ng.at[1, :, ca], n_fl), ROWS)
     n_last += [send(ng.at[1, :, ca], n_gl.at[:, ca], right)]
@@ -380,12 +393,14 @@
     n_fwd_l.wait_recv()
     merge_rows(ng.at[2, :, cb], (ng.at[2, :, cb], n_fr), ROWS)
     n_last += [send(ng.at[2, :, cb], n_gr.at[:, cb], left)]
+    z_0 = z_finish(0, *z_0)
+
     squares = jnp.zeros((PR, HP), F32)
     gains = jnp.zeros((PR, HP), F32)
     for q, copies in ((1, z_1), (0, z_0)):
         arrived(*copies)
         block = sblock(q, 0)[...].astype(F32)
-        for d in range(7):
+        for d in (0, 1, 2, 4, 5, 6):
             block = block + zd_in[q, d].astype(F32)
         cols = slice(q * HP, q * HP + HP)
         proj_out[:, cols] = block
@@ -497,7 +512,7 @@
             V((2, 4, 4, 2, PR, PC), BF16), V((2, 4, 4, PR, PC), BF16),
             V((2, 2, PR, PC), BF16), V((2, 2, PR, PC), BF16),
             V((2, 4, PR, PC), BF16), V((2, 4, PR, PC), BF16), V((2, 4, PR, PC), BF16),
-            V((2, 7, PR, HP), BF16),
+            V((2, 7, PR, HP), BF16), V((2, PR, HP), BF16),
             V((4, ROWS, DS), BF16), V((ROWS, HALF), BF16), V((ROWS, HALF), BF16),
             V((ROWS, DS), BF16), V((ROWS, DS), BF16),
             V((1, DS), F32), V((32, 128), F32), V((8, 128), F32), V((16, 128), F32),

time: 149 us -> 147 us (0.987)
  Pallas kernels: 148 us -> 146 us
    pallas_call x1, Pallas kernels: 145 us -> 143 us  [shards(): pl.pallas_call(kernel, out_shape=(jax.ShapeDtypeStruct((1, 128), F32), ja...]
where the time goes in v1:
time: 147 us
  Pallas kernels  146 us (99%)
    pallas_call x1, Pallas kernels, shards(): pl.pallas_call(kernel, out_shape=(jax.ShapeDtypeStruct((1, 128), F32), ja...  143 us
    pallas_call x1, Pallas kernels, shards(): pl.pallas_call(finish, out_shape=(jax.ShapeDtypeStruct((1, 128), F32), ja...  3.67 us

profile of v1, /device:TPU:1, one launch (start us, length us, event | category | flops | bytes accessed | tf_op | source)
XLA Modules:
  0.0 147.1 jit_solution(1574837618492021347)
XLA Ops:
  0.6 142.8 %shard_map.75 = (f32[1,128]{1,0:T(1,128)}, bf16[128,3584]{1,0:T(8,128)(2,1)}, f32[112,512]{1,0:T(8,128)}, f32[32,112]{1,0:T(8,128)}) custom-call(bf16[128,3584]{1,0:T(8,128)(2,1)} %hid.1, f32[3584]{0:T(1024)} %gain_in.1, bf16[112,512]{1,0:T(8,128)(2,1)} %proj.1, bf16[4,2,128,4096]{3,2,1,0:T(8,128)(2,1)} %bitcast.3), custom_call_target="tpu_custom_call" | custom-call | tf_op jit(solution)/shard_map/pallas_call | solution.py:491
  143.4 3.7 %shard_map.76 = (f32[1,128]{1,0:T(1,128)}, bf16[128,3584]{1,0:T(8,128)(2,1)}, f32[112,512]{1,0:T(8,128)}, f32[3584]{0:T(1024)}) custom-call(f32[1,128]{1,0:T(1,128)} %get-tuple-element.12.loss, bf16[128,3584]{1,0:T(8,128)(2,1)} %get-tuple-element.13.hid, f32[112,512]{1,0:T(8,128)} %get-tuple-element.14.proj, f32[32,112]{1,0:T(8,128)} %get-tuple-element.15.gain), custom_call_target="tpu_custom_call" | custom-call | tf_op jit(solution)/shard_map/pallas_call | solution.py:527
